TPU v7x, 512 devices: a whole 4x4x16 slice. The times are simulated.
512 devices in a mesh: seq: 128 (over x, z, core), head: 4 (over y).
Axes of the slice: x: 4, y: 4, z: 16, core: 2. Of those that a mesh axis runs over, the one named last changes fastest.
Arguments:
- tile_rows: bfloat16 [65536, 512], P('seq', 'head'), as said below
- tile_order: int32 [65536], P('seq'), may hold values from 0 to 65535, as said below
- tissue_mask: int32 [65536], P('seq'), may hold values from 0 to 1, as said below
- conv_weight: bfloat16 [512, 64, 512], P('seq', None, 'head'), may hold values from -0.03125 to 0.03125
- conv_bias: float32 [512], P('head'), may hold values from -3 to 3
- norm_gain: float32 [512], P('head'), may hold values from 0.1 to 1.9
- norm_bias: float32 [512], P('head'), may hold values from -3 to 3
- query_weight: bfloat16 [512, 512], P(None, 'head'), may hold values from -0.796875 to 0.796875
- key_weight: bfloat16 [512, 512], P(None, 'head'), may hold values from -0.25 to 0.25
- value_weight: bfloat16 [512, 512], P(None, 'head'), may hold values from -0.25 to 0.25
- out_weight: bfloat16 [512, 512], P('head'), may hold values from -0.25 to 0.25
Outputs:
- attention_out: bfloat16 [65536, 512], P('seq', 'head')
Inputs may be any that keep to these rules, and one draw needn't show every extreme that they name: `tile_rows`: features of the tiles. `tile_order`: A permutation of the grid positions. Grid blocks of 8 x 8 tiles are numbered row-major and owned in runs of 8 by the indices of seq in order; of the 512 tiles of one index of seq, at most 8 lie in the blocks of one owner, and every index of seq has 8 in the blocks of some owner. `tissue_mask`: 1 marks tissue, 0 background.
All inputs are finite; a program needn't handle non-finite values.
Results may differ from a plain program's by a relative error of at most 0.015.
The roundings to bfloat16 on the way count: a program that leaves them out, or rounds other values in their place, can miss the bound.
Values may be sent and summed in bfloat16 or wider, within the bound.
No kernel may reach another device: no remote copies, remote signals or barrier semaphores. Data moves between devices by JAX's collectives and lax.ppermute only.
A program may use at most 64 MiB of HBM per device.

v0:
```python
import math
import jax
import jax.numpy as jnp
from jax import lax
from jax.sharding import PartitionSpec as P

HEAD_SIZE = 64
REDUCE = 8
GRID_W = 512


def block_step(count):
    best = 1
    for candidate in range(1, min(count, 512) + 1):
        if count % candidate == 0:
            best = candidate
    return best


def make_fold(queries, heads_here, scale):

    def fold(carry, piece, start):
        count = piece.shape[0]
        step = block_step(count)
        blocks = piece.reshape(count // step, step, piece.shape[1])
        split_at = heads_here * HEAD_SIZE

        def visit(state, key_block):
            highest, totals, accum = state
            keys3 = key_block[:, :split_at].reshape(step, heads_here, HEAD_SIZE)
            values3 = key_block[:, split_at:].reshape(step, heads_here, HEAD_SIZE)
            scores = (
                jnp.einsum("thd,khd->htk", queries, keys3, preferred_element_type=jnp.float32)
                * scale
            )
            newest = jnp.maximum(highest, jnp.max(scores, -1))
            shrink = jnp.exp(highest - newest)
            weights = jnp.exp(scores - newest[:, :, None])
            totals = totals * shrink + jnp.sum(weights, -1)
            update = jnp.einsum(
                "htk,khd->thd",
                weights.astype(jnp.bfloat16),
                values3,
                preferred_element_type=jnp.float32,
            )
            accum = accum * shrink.T[:, :, None] + update
            return ((newest, totals, accum), None)

        carry, unused = lax.scan(visit, carry, blocks)
        return carry

    return fold


def local(
    tile_rows,
    tile_order,
    tissue_mask,
    conv_weight,
    conv_bias,
    norm_gain,
    norm_bias,
    query_weight,
    key_weight,
    value_weight,
    out_weight,
):
    devices = lax.axis_size("seq")
    local_rows, quarter = tile_rows.shape
    width = query_weight.shape[0]
    patch = conv_weight.shape[1]
    blocks_here = local_rows // patch
    capacity = 2 * (local_rows // devices)
    flags = tissue_mask.astype(jnp.bfloat16)
    masked = tile_rows * flags[:, None]
    grid_row = tile_order // GRID_W
    grid_col = tile_order % GRID_W
    block = grid_row // REDUCE * (GRID_W // REDUCE) + grid_col // REDUCE
    offset = grid_row % REDUCE * REDUCE + grid_col % REDUCE
    owner = block // blocks_here
    target = block % blocks_here * patch + offset
    onehot = (owner[:, None] == jnp.arange(devices, dtype=jnp.int32)[None, :]).astype(jnp.int32)
    ranks = jnp.sum(onehot * (jnp.cumsum(onehot, 0) - 1), 1)
    outgoing = jnp.zeros((devices, capacity, quarter), jnp.bfloat16).at[owner, ranks].set(masked)
    where_to = jnp.full((devices, capacity), -1, jnp.int32).at[owner, ranks].set(target)
    incoming, arrived = (
        lax.all_to_all(outgoing, "seq", split_axis=0, concat_axis=0, tiled=True),
        lax.all_to_all(where_to, "seq", split_axis=0, concat_axis=0, tiled=True),
    )
    places = arrived.reshape(-1)
    places = jnp.where(places >= 0, places, local_rows)
    patches = (
        jnp.zeros((local_rows + 1, quarter), jnp.bfloat16)
        .at[places]
        .set(incoming.reshape(-1, quarter))
    )
    patches = patches[:local_rows].reshape(blocks_here, patch, quarter)
    partial_conv = jnp.einsum(
        "bpc,opc->bo",
        patches,
        lax.all_gather(conv_weight, "seq", axis=0, tiled=True),
        preferred_element_type=jnp.float32,
    )
    shares = (
        lax.psum_scatter(partial_conv, "head", scatter_dimension=1, tiled=True) + conv_bias[None, :]
    )
    first_sum, second_sum = lax.psum((jnp.sum(shares, 1), jnp.sum(shares * shares, 1)), "head")
    center = (first_sum / width)[:, None]
    spread = (second_sum / width)[:, None]
    normed_share = (
        (shares - center) * lax.rsqrt(spread - center * center + 1e-05) * norm_gain + norm_bias
    ).astype(jnp.bfloat16)
    normed = lax.all_gather(normed_share, "head", axis=1, tiled=True)
    keys_here = jnp.dot(normed, key_weight, preferred_element_type=jnp.float32).astype(jnp.bfloat16)
    values_here = jnp.dot(normed, value_weight, preferred_element_type=jnp.float32).astype(
        jnp.bfloat16
    )
    key_value = jnp.concatenate([keys_here, values_here], 1)
    features = lax.all_gather(tile_rows, "head", axis=1, tiled=True)
    heads_here = quarter // HEAD_SIZE
    queries = jnp.dot(features, query_weight, preferred_element_type=jnp.float32).astype(
        jnp.bfloat16
    )
    queries = queries.reshape(local_rows, heads_here, HEAD_SIZE)
    scale = 1.0 / math.sqrt(HEAD_SIZE)
    start_state = (
        jnp.full((heads_here, local_rows), -1e30, jnp.float32),
        jnp.zeros((heads_here, local_rows), jnp.float32),
        jnp.zeros((local_rows, heads_here, HEAD_SIZE), jnp.float32),
    )
    folder = make_fold(queries, heads_here, scale)
    every_key = lax.all_gather(key_value, "seq", axis=0, tiled=True)
    highest, totals, accum = folder(start_state, every_key, 0)
    attended = (accum / totals.T[:, :, None]).reshape(local_rows, quarter).astype(jnp.bfloat16)
    projected = jnp.dot(attended, out_weight, preferred_element_type=jnp.float32)
    summed = lax.psum_scatter(
        projected.astype(jnp.bfloat16), "head", scatter_dimension=1, tiled=True
    ).astype(jnp.float32)
    return (summed * tissue_mask[:, None].astype(jnp.float32)).astype(jnp.bfloat16)


def solution(mesh):
    return jax.shard_map(
        local,
        mesh=mesh,
        in_specs=(
            P("seq", "head"),
            P("seq"),
            P("seq"),
            P("seq", None, "head"),
            P("head"),
            P("head"),
            P("head"),
            P(None, "head"),
            P(None, "head"),
            P(None, "head"),
            P("head", None),
        ),
        out_specs=P("seq", "head"),
        check_vma=False,
    )
```

profile of v0, /device:TPU:2, one launch (start us, length us, event | category | flops | bytes accessed | tf_op | source)
XLA Modules:
  0.0 349.9 jit_solution(16431818356530717991)
XLA Ops:
  6.5 0.7 all-gather.2.cloned.1.call-update
  8.7 22.0 %scatter_fusion = s32[128,8]{0,1:T(8,128)S(1)} fusion(s32[128,8]{0,1:T(8,128)S(1)} %broadcast_in_dim.22, s32[512]{0:T(512)S(1)} %bitcast.79, s32[512]{0:T(512)S(1)} %get-tuple-element.97), kind=kCustom, calls=%fused_computation | custom fusion | bytes 10240 | tf_op jit(solution)/shard_map/scatter | solution.py:85
  30.7 0.7 copy.25
  31.5 19.5 %all-to-all-start = ((s32[128,1,8]{2,1,0:T(1,128)}), s32[128,1,8]{2,1,0:T(1,128)S(1)}, u32[]{:S(2)}, u32[]{:S(2)}) async-start(s32[128,1,8]{2,1,0:T(1,128)} %copy.25), calls=%async_computation | async-start | bytes 131072 | tf_op jit(solution)/shard_map/all_to_all | solution.py:88
  51.2 0.7 broadcast_in_dim.48
  51.9 51.3 %scatter_fusion.1 = bf16[128,8,128]{2,1,0:T(8,128)(2,1)} fusion(bf16[128,8,128]{2,1,0:T(8,128)(2,1)} %broadcast_in_dim.48, s32[512]{0:T(512)S(1)} %bitcast.80, bf16[512,128]{1,0:T(8,128)(2,1)S(1)} %broadcast_multiply_fusion), kind=kCustom, calls=%fused_computation.1 | custom fusion | bytes 397312 | tf_op jit(solution)/shard_map/scatter | solution.py:84
  103.3 16.2 %all-to-all-start.1 = ((bf16[128,8,128]{2,1,0:T(8,128)(2,1)}), bf16[128,8,128]{2,1,0:T(8,128)(2,1)S(1)}, u32[]{:S(2)}, u32[]{:S(2)}) async-start(bf16[128,8,128]{2,1,0:T(8,128)(2,1)} %scatter_fusion.1), calls=%async_computation.1 | async-start | bytes 524288 | tf_op jit(solution)/shard_map/all_to_all | solution.py:87
  119.5 14.0 %all_gather.15 = bf16[512,512]{1,0:T(8,128)(2,1)S(1)} all-gather(bf16[512,128]{1,0:T(8,128)(2,1)S(1)} %copy-done.1), channel_id=1, replica_groups=mesh['seq'=128,'head'=4] {'head'}, dimensions={1}, use_global_device_ids=true | all-gather | bytes 655360 | tf_op jit(solution)/shard_map/all_gather | solution.py:119
  134.0 0.8 reduce.3
  135.0 9.7 %all-to-all-done.1 = bf16[128,8,128]{2,1,0:T(8,128)(2,1)S(1)} async-done(((bf16[128,8,128]{2,1,0:T(8,128)(2,1)}), bf16[128,8,128]{2,1,0:T(8,128)(2,1)S(1)}, u32[]{:S(2)}, u32[]{:S(2)}) %all-to-all-start.1) | async-done | bytes 262176 | tf_op jit(solution)/shard_map/all_to_all | solution.py:87
  144.7 3.4 scatter_custom_fusion.2
  148.1 20.0 %all-gather.2.cloned.1.call-done = bf16[512,64,128]{2,1,0:T(8,128)(2,1)} async-done(((bf16[4,64,128]{2,1,0:T(8,128)(2,1)}), bf16[512,64,128]{2,1,0:T(8,128)(2,1)}) %all-gather.2.cloned.1.call-update) | async-done | bytes 8388624 | tf_op jit(solution)/shard_map/all_gather | solution.py:101
  168.1 12.4 %fusion.13 = f32[8,512]{1,0:T(8,128)} fusion(bf16[512,64,128]{2,1,0:T(8,128)(2,1)} %all-gather.2.cloned.1.call-done, bf16[8,64,128]{2,1,0:T(8,128)(2,1)S(1)} %bitcast.87), kind=kOutput, calls=%fused_computation.25 | convolution fusion | flops 67108864 | bytes 8536064 | tf_op jit(solution)/shard_map/bpc,opc->bo/dot_general | solution.py:98
  181.0 24.1 %reduce-scatter.5.cloned.1.call-done = f32[8,128]{1,0:T(8,128)} async-done(((f32[8,512]{1,0:T(8,128)}), f32[8,128]{1,0:T(8,128)}) %reduce-scatter.5.cloned.1.call-update) | async-done | bytes 4112 | tf_op jit(solution)/shard_map/reduce_scatter | solution.py:105
  205.0 0.8 add_reduce_fusion
  205.9 8.6 %all-reduce = (f32[8]{0:T(128)S(1)}, f32[8]{0:T(128)S(1)}) all-reduce(f32[8]{0:T(128)S(1)} %get-tuple-element.80, f32[8]{0:T(128)S(1)} %get-tuple-element.79), channel_id=1, replica_groups=mesh['seq'=128,'head'=4] {'head'}, use_global_device_ids=true, to_apply=%region_10.11 | all-reduce | flops 16 | bytes 128 | tf_op jit(solution)/shard_map/psum | solution.py:107
  214.4 0.8 add_convert_fusion
  215.2 10.4 %all_gather.13 = bf16[8,512]{1,0:T(8,128)(2,1)S(1)} all-gather(bf16[8,128]{1,0:T(8,128)(2,1)S(1)} %add_convert_fusion), channel_id=1, replica_groups=mesh['seq'=128,'head'=4] {'head'}, dimensions={1}, use_global_device_ids=true | all-gather | bytes 10240 | tf_op jit(solution)/shard_map/all_gather | solution.py:113
  225.8 84.1 %all_gather.14 = bf16[1024,256]{1,0:T(8,128)(2,1)S(1)} all-gather(bf16[8,256]{1,0:T(8,128)(2,1)S(1)} %pad_maximum_fusion), channel_id=1, replica_groups=mesh['seq'=128,'head'=4] {'seq'}, dimensions={0}, use_global_device_ids=true | all-gather | bytes 528384 | tf_op jit(solution)/shard_map/all_gather | solution.py:132
  309.9 3.3 while.15
  313.6 1.0 copy.30
  314.6 26.9 %reduce-scatter.7.cloned.1.call-done = bf16[128,512]{1,0:T(8,128)(2,1)} async-done(((bf16[512,512]{1,0:T(8,128)(2,1)}), bf16[128,512]{1,0:T(8,128)(2,1)}) %reduce-scatter.7.cloned.1.call-update) | async-done | bytes 131088
  341.6 1.0 copy.31
  342.6 0.8 multiply_convert_fusion
  (70 shorter events, 6.4 us)
Async XLA Ops:
  6.5 306.7 %copy-start = (bf16[128,512]{1,0:T(8,128)(2,1)S(1)}, bf16[128,512]{1,0:T(8,128)(2,1)}, u32[]{:S(2)}) copy-start(bf16[128,512]{1,0:T(8,128)(2,1)} %param.23) | copy-start | bytes 393220
  6.5 161.6 %all-gather.2.cloned.1.call-start = ((), (), s32[]{:S(2)}) async-start(), calls=%async_computation.4 | async-start | bytes 8454144 | tf_op jit(solution)/shard_map/all_gather | solution.py:101
  8.7 42.3 %copy-start.5 = (s32[512]{0:T(512)S(1)}, s32[512]{0:T(512)}, u32[]{:S(2)}) copy-start(s32[512]{0:T(512)} %param.15) | copy-start | bytes 6148
  8.7 42.3 %copy-start.1 = (bf16[512,128]{1,0:T(8,128)(2,1)S(1)}, bf16[512,128]{1,0:T(8,128)(2,1)}, u32[]{:S(2)}) copy-start(bf16[512,128]{1,0:T(8,128)(2,1)} %param.13) | copy-start | bytes 393220
  31.5 71.8 %all-to-all-start = ((s32[128,1,8]{2,1,0:T(1,128)}), s32[128,1,8]{2,1,0:T(1,128)S(1)}, u32[]{:S(2)}, u32[]{:S(2)}) async-start(s32[128,1,8]{2,1,0:T(1,128)} %copy.25), calls=%async_computation | async-start | bytes 131072 | tf_op jit(solution)/shard_map/all_to_all | solution.py:88
  103.3 41.4 %all-to-all-start.1 = ((bf16[128,8,128]{2,1,0:T(8,128)(2,1)}), bf16[128,8,128]{2,1,0:T(8,128)(2,1)S(1)}, u32[]{:S(2)}, u32[]{:S(2)}) async-start(bf16[128,8,128]{2,1,0:T(8,128)(2,1)} %scatter_fusion.1), calls=%async_computation.1 | async-start | bytes 524288 | tf_op jit(solution)/shard_map/all_to_all | solution.py:87
  119.4 85.6 %reduce-scatter.5.cloned.1.call-start = ((), (), s32[]{:S(2)}) async-start(), calls=%async_computation.5 | async-start | bytes 20480 | tf_op jit(solution)/shard_map/reduce_scatter | solution.py:105
  168.1 12.5 %copy-start.4 = (bf16[512,128]{1,0:T(8,128)(2,1)S(1)}, bf16[512,128]{1,0:T(8,128)(2,1)}, u32[]{:S(2)}) copy-start(bf16[512,128]{1,0:T(8,128)(2,1)} %param.20) | copy-start | bytes 393220
  168.1 36.9 %copy-start.6 = (f32[128]{0:T(128)S(1)}, f32[128]{0:T(128)}, u32[]{:S(2)}) copy-start(f32[128]{0:T(128)} %param.17) | copy-start | bytes 1540
  168.1 46.3 %copy-start.7 = (f32[128]{0:T(128)S(1)}, f32[128]{0:T(128)}, u32[]{:S(2)}) copy-start(f32[128]{0:T(128)} %param.19) | copy-start | bytes 1540
  168.1 46.3 %copy-start.8 = (f32[128]{0:T(128)S(1)}, f32[128]{0:T(128)}, u32[]{:S(2)}) copy-start(f32[128]{0:T(128)} %param.18) | copy-start | bytes 1540
  168.1 57.5 %copy-start.2 = (bf16[512,128]{1,0:T(8,128)(2,1)S(1)}, bf16[512,128]{1,0:T(8,128)(2,1)}, u32[]{:S(2)}) copy-start(bf16[512,128]{1,0:T(8,128)(2,1)} %param.22) | copy-start | bytes 393220
  168.1 57.6 %copy-start.3 = (bf16[512,128]{1,0:T(8,128)(2,1)S(1)}, bf16[512,128]{1,0:T(8,128)(2,1)}, u32[]{:S(2)}) copy-start(bf16[512,128]{1,0:T(8,128)(2,1)} %param.21) | copy-start | bytes 393220
  180.6 161.0 %reduce-scatter.7.cloned.1.call-start = ((), (), s32[]{:S(2)}) async-start(), calls=%async_computation.6 | async-start | bytes 655360
Sparse Core Ops, SparseCore 0:
  10.5 157.5 all-gather.1
  180.7 24.3 reduce-scatter.4
  314.7 26.7 reduce-scatter.6
where the time goes:
time: 351 us; the launch traced here: 350 us
  blocking collectives  117 us (33%)
  waiting for transfers between devices  81.5 us (23%)
  local copies, waits for them, and re-layouts  81.4 us (23%)
  starting transfers between devices  35.8 us (10%)
  matrix products  15.3 us (4%)
  between operations  13.4 us (4%)
  other arithmetic  5.44 us (2%)
    all_gather x1, blocking collectives, local(): every_key = lax.all_gather(key_value, 'seq', axis=0, tiled=True)  84.1 us
    scatter x1, local copies, waits for them, and re-layouts, local(): jnp.zeros((devices, capacity, quarter), jnp.bfloat16).at[owner, ranks]  51.3 us
    unnamed x4, waiting for transfers between devices  27.7 us
    reduce_scatter x1, waiting for transfers between devices, local(): lax.psum_scatter(partial_conv, 'head', scatter_dimension=1, tiled=True)  24.1 us
    scatter x1, local copies, waits for them, and re-layouts, local(): jnp.full((devices, capacity), -1, jnp.int32).at[owner, ranks].set(target)  22 us
    all_gather x1, waiting for transfers between devices, local(): lax.all_gather(conv_weight, 'seq', axis=0, tiled=True)  20 us
    all_to_all x1, starting transfers between devices, local(): lax.all_to_all(where_to, 'seq', split_axis=0, concat_axis=0, tiled=True)  19.5 us
    all_to_all x1, starting transfers between devices, local(): lax.all_to_all(outgoing, 'seq', split_axis=0, concat_axis=0, tiled=True)  16.2 us
  transfers between devices with their start and end apart: 5, of which 4 were waited for; matrix products, arithmetic and copies ran while one was open for 23% of the time, Pallas kernels for 0%

commit v1 on v0

--- a/solution.py
+++ b/solution.py
@@ -129,7 +129,8 @@
         jnp.zeros((local_rows, heads_here, HEAD_SIZE), jnp.float32),
     )
     folder = make_fold(queries, heads_here, scale)
-    every_key = lax.all_gather(key_value, "seq", axis=0, tiled=True)
+    sent = jnp.stack([key_value] * lax.axis_size("seq"))
+    every_key = jnp.concatenate(lax.all_to_all(sent, "seq", 0, 0), axis=0)
     highest, totals, accum = folder(start_state, every_key, 0)
     attended = (accum / totals.T[:, :, None]).reshape(local_rows, quarter).astype(jnp.bfloat16)
     projected = jnp.dot(attended, out_weight, preferred_element_type=jnp.float32)

time: 351 us -> 311 us (0.89)
  blocking collectives: 117 us -> 33 us
  waiting for transfers between devices: 81.5 us -> 108 us
  starting transfers between devices: 35.8 us -> 52.4 us
    all_gather x1 -> x0, blocking collectives: 84.1 us -> none  [local(): every_key = lax.all_gather(key_value, 'seq', axis=0, tiled=True)]
    all_to_all x0 -> x1, waiting for transfers between devices: none -> 19.2 us  [local(): every_key = jnp.concatenate(lax.all_to_all(sent, 'seq', 0, 0), axis=0)]
    all_to_all x0 -> x1, starting transfers between devices: none -> 16.6 us  [local(): every_key = jnp.concatenate(lax.all_to_all(sent, 'seq', 0, 0), axis=0)]
    all_to_all x1, waiting for transfers between devices: 9.73 us -> 23.8 us  [local(): lax.all_to_all(outgoing, 'seq', split_axis=0, concat_axis=0, tiled=True)]
    unnamed x4, waiting for transfers between devices: 27.7 us -> 20.9 us
  transfers between devices with their start and end apart: 5 -> 6, of which waited for: 4 -> 5; matrix products, arithmetic and copies ran while one was open for 23% -> 26% of each run, Pallas kernels for 0% -> 0%
where the time goes in v1:
time: 311 us; the launch traced here: 310 us
  waiting for transfers between devices  108 us (35%)
  local copies, waits for them, and re-layouts  82.2 us (26%)
  starting transfers between devices  52.4 us (17%)
  blocking collectives  33 us (11%)
  matrix products  15.3 us (5%)
  between operations  13.4 us (4%)
  other arithmetic  5.44 us (2%)
    scatter x1, local copies, waits for them, and re-layouts, local(): jnp.zeros((devices, capacity, quarter), jnp.bfloat16).at[owner, ranks]  51.3 us
    reduce_scatter x1, waiting for transfers between devices, local(): lax.psum_scatter(partial_conv, 'head', scatter_dimension=1, tiled=True)  24.5 us
    all_to_all x1, waiting for transfers between devices, local(): lax.all_to_all(outgoing, 'seq', split_axis=0, concat_axis=0, tiled=True)  23.8 us
    scatter x1, local copies, waits for them, and re-layouts, local(): jnp.full((devices, capacity), -1, jnp.int32).at[owner, ranks].set(target)  22 us
    unnamed x4, waiting for transfers between devices  20.9 us
    all_gather x1, waiting for transfers between devices, local(): lax.all_gather(conv_weight, 'seq', axis=0, tiled=True)  20 us
    all_to_all x1, starting transfers between devices, local(): lax.all_to_all(where_to, 'seq', split_axis=0, concat_axis=0, tiled=True)  19.5 us
    all_to_all x1, waiting for transfers between devices, local(): every_key = jnp.concatenate(lax.all_to_all(sent, 'seq', 0, 0), axis=0)  19.2 us
  transfers between devices with their start and end apart: 6, of which 5 were waited for; matrix products, arithmetic and copies ran while one was open for 26% of the time, Pallas kernels for 0%

profile of v1, /device:TPU:2, one launch (start us, length us, event | category | flops | bytes accessed | tf_op | source)
XLA Modules:
  0.0 310.1 jit_solution(6646319603645169918)
XLA Ops:
  8.7 22.0 %scatter_fusion = s32[128,8]{0,1:T(8,128)S(1)} fusion(s32[128,8]{0,1:T(8,128)S(1)} %broadcast_in_dim.22, s32[512]{0:T(512)S(1)} %bitcast.79, s32[512]{0:T(512)S(1)} %get-tuple-element.91), kind=kCustom, calls=%fused_computation | custom fusion | bytes 10240 | tf_op jit(solution)/shard_map/scatter | solution.py:85
  31.5 19.5 %all-to-all-start = ((s32[128,1,8]{2,1,0:T(1,128)}), s32[128,1,8]{2,1,0:T(1,128)S(1)}, u32[]{:S(2)}, u32[]{:S(2)}) async-start(s32[128,1,8]{2,1,0:T(1,128)} %copy.24), calls=%async_computation | async-start | bytes 131072 | tf_op jit(solution)/shard_map/all_to_all | solution.py:88
  51.2 0.7 broadcast_in_dim.48
  51.9 51.3 %scatter_fusion.1 = bf16[128,8,128]{2,1,0:T(8,128)(2,1)} fusion(bf16[128,8,128]{2,1,0:T(8,128)(2,1)} %broadcast_in_dim.48, s32[512]{0:T(512)S(1)} %bitcast.80, bf16[512,128]{1,0:T(8,128)(2,1)S(1)} %broadcast_multiply_fusion), kind=kCustom, calls=%fused_computation.1 | custom fusion | bytes 397312 | tf_op jit(solution)/shard_map/scatter | solution.py:84
  103.3 16.2 %all-to-all-start.1 = ((bf16[128,8,128]{2,1,0:T(8,128)(2,1)}), bf16[128,8,128]{2,1,0:T(8,128)(2,1)S(1)}, u32[]{:S(2)}, u32[]{:S(2)}) async-start(bf16[128,8,128]{2,1,0:T(8,128)(2,1)} %scatter_fusion.1), calls=%async_computation.1 | async-start | bytes 524288 | tf_op jit(solution)/shard_map/all_to_all | solution.py:87
  120.0 0.8 reduce.3
  120.9 23.8 %all-to-all-done.1 = bf16[128,8,128]{2,1,0:T(8,128)(2,1)S(1)} async-done(((bf16[128,8,128]{2,1,0:T(8,128)(2,1)}), bf16[128,8,128]{2,1,0:T(8,128)(2,1)S(1)}, u32[]{:S(2)}, u32[]{:S(2)}) %all-to-all-start.1) | async-done | bytes 262176 | tf_op jit(solution)/shard_map/all_to_all | solution.py:87
  144.7 3.4 %scatter_custom_fusion.2 = bf16[513,128]{1,0:T(8,128)(2,1)S(1)} fusion(s32[1024]{0:T(1024)S(1)} %bitcast.94, bf16[128,8,128]{2,1,0:T(8,128)(2,1)S(1)} %all-to-all-done.1, bf16[]{:T(256)} %constant.103.clone.1), kind=kCustom, calls=%fused_computation.30 | custom fusion | bytes 393474 | tf_op jit(solution)/shard_map/scatter | solution.py:95
  148.1 20.0 %all-gather.2.cloned.1.call-done = bf16[512,64,128]{2,1,0:T(8,128)(2,1)} async-done(((bf16[4,64,128]{2,1,0:T(8,128)(2,1)}), bf16[512,64,128]{2,1,0:T(8,128)(2,1)}) %all-gather.2.cloned.1.call-update) | async-done | bytes 8388624 | tf_op jit(solution)/shard_map/all_gather | solution.py:101
  168.1 12.4 %fusion.13 = f32[8,512]{1,0:T(8,128)} fusion(bf16[512,64,128]{2,1,0:T(8,128)(2,1)} %all-gather.2.cloned.1.call-done, bf16[8,64,128]{2,1,0:T(8,128)(2,1)S(1)} %bitcast.87), kind=kOutput, calls=%fused_computation.25 | convolution fusion | flops 67108864 | bytes 8536064 | tf_op jit(solution)/shard_map/bpc,opc->bo/dot_general | solution.py:98
  180.5 24.5 %reduce-scatter.5.cloned.1.call-done = f32[8,128]{1,0:T(8,128)} async-done(((f32[8,512]{1,0:T(8,128)}), f32[8,128]{1,0:T(8,128)}) %reduce-scatter.5.cloned.1.call-update) | async-done | bytes 4112 | tf_op jit(solution)/shard_map/reduce_scatter | solution.py:105
  205.0 0.8 add_reduce_fusion
  205.8 8.6 %all-reduce = (f32[8]{0:T(128)S(1)}, f32[8]{0:T(128)S(1)}) all-reduce(f32[8]{0:T(128)S(1)} %get-tuple-element.74, f32[8]{0:T(128)S(1)} %get-tuple-element.73), channel_id=1, replica_groups=mesh['seq'=128,'head'=4] {'head'}, use_global_device_ids=true, to_apply=%region_10.11 | all-reduce | flops 16 | bytes 128 | tf_op jit(solution)/shard_map/psum | solution.py:107
  214.4 0.8 add_convert_fusion
  215.2 10.4 %all_gather.10 = bf16[8,512]{1,0:T(8,128)(2,1)S(1)} all-gather(bf16[8,128]{1,0:T(8,128)(2,1)S(1)} %add_convert_fusion), channel_id=1, replica_groups=mesh['seq'=128,'head'=4] {'head'}, dimensions={1}, use_global_device_ids=true | all-gather | bytes 10240 | tf_op jit(solution)/shard_map/all_gather | solution.py:113
  225.8 0.8 stack.2
  226.6 16.6 %all-to-all-start.2 = ((bf16[128,8,256]{2,1,0:T(8,128)(2,1)}), bf16[128,8,256]{2,1,0:T(8,128)(2,1)S(1)}, u32[]{:S(2)}, u32[]{:S(2)}) async-start(bf16[128,8,256]{2,1,0:T(8,128)(2,1)} %stack.2), calls=%async_computation.3 | async-start | bytes 1048576 | tf_op jit(solution)/shard_map/all_to_all | solution.py:133
  243.3 14.0 %all_gather.11 = bf16[512,512]{1,0:T(8,128)(2,1)S(1)} all-gather(bf16[512,128]{1,0:T(8,128)(2,1)S(1)} %copy-done.1), channel_id=1, replica_groups=mesh['seq'=128,'head'=4] {'head'}, dimensions={1}, use_global_device_ids=true | all-gather | bytes 655360 | tf_op jit(solution)/shard_map/all_gather | solution.py:119
  257.7 19.2 %all-to-all-done.2 = bf16[128,8,256]{2,1,0:T(8,128)(2,1)S(1)} async-done(((bf16[128,8,256]{2,1,0:T(8,128)(2,1)}), bf16[128,8,256]{2,1,0:T(8,128)(2,1)S(1)}, u32[]{:S(2)}, u32[]{:S(2)}) %all-to-all-start.2) | async-done | bytes 524320 | tf_op jit(solution)/shard_map/all_to_all | solution.py:133
  276.9 3.3 %while.15 = (s32[]{:T(128)}, f32[2,512]{1,0:T(2,128)S(1)}, f32[2,512]{1,0:T(2,128)S(1)}, f32[512,2,64]{0,2,1:T(8,128)S(1)}, bf16[2,512,256]{2,1,0:T(8,128)(2,1)S...) while((s32[]{:T(128)}, f32[2,512]{1,0:T(2,128)S(1)}, f32[2,512]{1,0:T(2,128)S(1)}, ...), condition=%wide.region_14.15_spmd.clone, body=%wide.region_11.14_spmd.clone.sunk | while | flops 138614784 | bytes 8847461 | solution.py:49
  280.6 1.0 copy.29
  281.6 20.1 %reduce-scatter.7.cloned.1.call-done = bf16[128,512]{1,0:T(8,128)(2,1)} async-done(((bf16[512,512]{1,0:T(8,128)(2,1)}), bf16[128,512]{1,0:T(8,128)(2,1)}) %reduce-scatter.7.cloned.1.call-update) | async-done | bytes 131088
  301.7 1.0 copy.30
  302.7 0.8 multiply_convert_fusion
  (72 shorter events, 7.9 us)
Async XLA Ops:
  6.5 273.7 %copy-start = (bf16[128,512]{1,0:T(8,128)(2,1)S(1)}, bf16[128,512]{1,0:T(8,128)(2,1)}, u32[]{:S(2)}) copy-start(bf16[128,512]{1,0:T(8,128)(2,1)} %param.23) | copy-start | bytes 393220
  6.5 161.6 %all-gather.2.cloned.1.call-start = ((), (), s32[]{:S(2)}) async-start(), calls=%async_computation.5 | async-start | bytes 8454144 | tf_op jit(solution)/shard_map/all_gather | solution.py:101
  8.7 42.3 %copy-start.5 = (s32[512]{0:T(512)S(1)}, s32[512]{0:T(512)}, u32[]{:S(2)}) copy-start(s32[512]{0:T(512)} %param.15) | copy-start | bytes 6148
  8.7 42.3 %copy-start.1 = (bf16[512,128]{1,0:T(8,128)(2,1)S(1)}, bf16[512,128]{1,0:T(8,128)(2,1)}, u32[]{:S(2)}) copy-start(bf16[512,128]{1,0:T(8,128)(2,1)} %param.13) | copy-start | bytes 393220
  31.5 71.8 %all-to-all-start = ((s32[128,1,8]{2,1,0:T(1,128)}), s32[128,1,8]{2,1,0:T(1,128)S(1)}, u32[]{:S(2)}, u32[]{:S(2)}) async-start(s32[128,1,8]{2,1,0:T(1,128)} %copy.24), calls=%async_computation | async-start | bytes 131072 | tf_op jit(solution)/shard_map/all_to_all | solution.py:88
  103.3 41.4 %all-to-all-start.1 = ((bf16[128,8,128]{2,1,0:T(8,128)(2,1)}), bf16[128,8,128]{2,1,0:T(8,128)(2,1)S(1)}, u32[]{:S(2)}, u32[]{:S(2)}) async-start(bf16[128,8,128]{2,1,0:T(8,128)(2,1)} %scatter_fusion.1), calls=%async_computation.1 | async-start | bytes 524288 | tf_op jit(solution)/shard_map/all_to_all | solution.py:87
  119.4 85.6 %reduce-scatter.5.cloned.1.call-start = ((), (), s32[]{:S(2)}) async-start(), calls=%async_computation.6 | async-start | bytes 20480 | tf_op jit(solution)/shard_map/reduce_scatter | solution.py:105
  168.1 36.9 %copy-start.6 = (f32[128]{0:T(128)S(1)}, f32[128]{0:T(128)}, u32[]{:S(2)}) copy-start(f32[128]{0:T(128)} %param.17) | copy-start | bytes 1540
  168.1 46.3 %copy-start.7 = (f32[128]{0:T(128)S(1)}, f32[128]{0:T(128)}, u32[]{:S(2)}) copy-start(f32[128]{0:T(128)} %param.19) | copy-start | bytes 1540
  168.1 46.3 %copy-start.8 = (f32[128]{0:T(128)S(1)}, f32[128]{0:T(128)}, u32[]{:S(2)}) copy-start(f32[128]{0:T(128)} %param.18) | copy-start | bytes 1540
  168.1 57.4 %copy-start.2 = (bf16[512,128]{1,0:T(8,128)(2,1)S(1)}, bf16[512,128]{1,0:T(8,128)(2,1)}, u32[]{:S(2)}) copy-start(bf16[512,128]{1,0:T(8,128)(2,1)} %param.22) | copy-start | bytes 393220
  168.1 57.6 %copy-start.3 = (bf16[512,128]{1,0:T(8,128)(2,1)S(1)}, bf16[512,128]{1,0:T(8,128)(2,1)}, u32[]{:S(2)}) copy-start(bf16[512,128]{1,0:T(8,128)(2,1)} %param.21) | copy-start | bytes 393220
  180.5 76.9 %copy-start.4 = (bf16[512,128]{1,0:T(8,128)(2,1)S(1)}, bf16[512,128]{1,0:T(8,128)(2,1)}, u32[]{:S(2)}) copy-start(bf16[512,128]{1,0:T(8,128)(2,1)} %param.20) | copy-start | bytes 393220
  226.6 50.2 %all-to-all-start.2 = ((bf16[128,8,256]{2,1,0:T(8,128)(2,1)}), bf16[128,8,256]{2,1,0:T(8,128)(2,1)S(1)}, u32[]{:S(2)}, u32[]{:S(2)}) async-start(bf16[128,8,256]{2,1,0:T(8,128)(2,1)} %stack.2), calls=%async_computation.3 | async-start | bytes 1048576 | tf_op jit(solution)/shard_map/all_to_all | solution.py:133
  243.3 58.5 %reduce-scatter.7.cloned.1.call-start = ((), (), s32[]{:S(2)}) async-start(), calls=%async_computation.7 | async-start | bytes 655360
Sparse Core Ops, SparseCore 0:
  10.5 157.5 all-gather.1
  180.6 24.3 reduce-scatter.4
  281.7 19.9 reduce-scatter.6
